TPU v7x, 256 devices: a whole 4x4x8 slice. The times are simulated.
256 devices in a mesh: fsdp: 8 (over y_lo, x), sp: 32 (over y_hi, z, core).
Axes of the slice: x: 4, y: 4 (y_hi: 2, y_lo: 2; y = y_hi * 2 + y_lo), z: 8, core: 2. Of those that a mesh axis runs over, the one named last changes fastest.
Arguments:
- queries: bfloat16 [24576, 3072], P('sp', 'fsdp'), may hold values from -6 to 6
- keys: bfloat16 [24576, 3072], P('sp', 'fsdp'), may hold values from -6 to 6
- values: bfloat16 [24576, 3072], P('sp', 'fsdp'), may hold values from -6 to 6
- w_out: bfloat16 [3072, 3072], P('fsdp', 'sp'), may hold values from -0.109375 to 0.109375
- grad_out: bfloat16 [24576, 3072], P('sp', 'fsdp'), may hold values from -6 to 6
- neighbors: int32 [64, 5], P('sp'), may hold values from -1 to 63, as said below
Outputs:
- output: bfloat16 [24576, 3072], P('sp', 'fsdp')
- grad_queries: bfloat16 [24576, 3072], P('sp', 'fsdp')
- grad_keys: bfloat16 [24576, 3072], P('sp', 'fsdp')
- grad_values: bfloat16 [24576, 3072], P('sp', 'fsdp')
- grad_weight: float32 [3072, 3072], P('fsdp', 'sp')
Inputs may be any that keep to these rules, and one draw needn't show every extreme that they name: `neighbors`: row t lists first, in ascending order, the distinct tiles that the queries of tile t attend to, each within 2 tiles of t and t itself always among them, then -1 in the unused slots; some row fills all 5 slots. Where they exist, tile t - 1 is listed for every t that is a multiple of 2, and tile t + 1 for every t one less than a multiple of 2.
All inputs are finite; a program needn't handle non-finite values.
Results may differ from a plain program's by a relative error of at most 0.02.
Values may be sent and summed in bfloat16 or wider, within the bound.
A program may use at most 128 MiB of HBM per device.

v0:
```python
import math

import jax
import jax.numpy as jnp
from jax import lax
from jax.experimental import pallas as pl
from jax.experimental.pallas import tpu as pltpu
from jax.sharding import PartitionSpec as P

HD = 128
TILE = 384
HEADS = 3
TOK = 768
COLS = 384
WIN = 5 * TILE
WIDE = 6 * TILE
PIECE = 96
MESH = pl.DeviceIdType.MESH
SCALE = 1.0 / math.sqrt(HD)
LOG2E = 1.4426950408889634
NEG_FILL = -1e30
BF = jnp.bfloat16
F32 = jnp.float32


def dot_nn(a, b):
    return lax.dot_general(a, b, (((1,), (0,)), ((), ())), preferred_element_type=F32)


def dot_nt(a, b):
    return lax.dot_general(a, b, (((1,), (1,)), ((), ())), preferred_element_type=F32)


def dot_tn(a, b):
    return lax.dot_general(a, b, (((0,), (0,)), ((), ())), preferred_element_type=F32)


def aligned(start, size):
    return pl.ds(pl.multiple_of(start, size), size)


def kernel(
    nb_ref, q_ref, k_ref, v_ref, w_ref, go_ref,
    out_ref, gq_ref, gk_ref, gv_ref, gw_ref,
    kw, vw, gall, wt, att, scores, probs, inv_total,
    gsend, grecv, gown, gatt,
    osend, orecv, oown, held,
    gw, cs, cr, rs_s, rs_r, ls_s, ls_r, ys, yr,
    dka, dva, hs, hr,
    local_sem, wy_s, wy_r, wr_s, wr_r, wl_s, wl_r, wc_s, wc_r,
    kv_s, kv_r, ga_s, ga_r, gf_s, gf_r, at_s, at_r, gr_s, gr_r, or_s, or_r,
    gc_s, gc_r, gright_s, gright_r, gleft_s, gleft_r, gy_s, gy_r, hk_s, hk_r,
):
    f = lax.axis_index("fsdp")
    s = lax.axis_index("sp")
    ylo, x = f // 4, f % 4
    yhi, z, core = s // 16, (s // 2) % 8, s % 2

    def device(ylo_at, x_at, yhi_at, z_at, core_at):
        return (ylo_at * 4 + x_at, yhi_at * 16 + z_at * 2 + core_at)

    z_next = device(ylo, x, yhi, (z + 1) % 8, core)
    z_prev = device(ylo, x, yhi, (z + 7) % 8, core)
    partner = device(ylo, x, yhi, z, 1 - core)
    y_partner = device(1 - ylo, x, yhi, z, core)
    sp_next = (f, (s + 1) % 32)
    sp_prev = (f, (s + 31) % 32)

    def x_at(k):
        return device(ylo, (x + k) % 4, yhi, z, core)

    def remote(src, dst, send, recv, to):
        return pltpu.make_async_remote_copy(
            src_ref=src, dst_ref=dst, send_sem=send, recv_sem=recv, device_id=to, device_id_type=MESH
        )

    barrier = pltpu.get_barrier_semaphore()
    greeted = [
        z_next, z_prev, partner, sp_next, sp_prev, y_partner,
        device(ylo, x, 1 - yhi, z, core), device(1 - ylo, x, 1 - yhi, z, core),
        x_at(1), x_at(2), x_at(3),
    ]
    for other in greeted:
        pl.semaphore_signal(barrier, inc=1, device_id=other, device_id_type=MESH)
    pl.semaphore_wait(barrier, len(greeted))

    def slot(z_at, core_at):
        return pl.ds(pl.multiple_of((z_at * 2 + core_at) * PIECE, 32), PIECE)

    w_lanes = aligned(ylo * COLS, 128 * 3)

    def w_out_copy(k):
        return remote(
            w_ref, wt.at[slot(z, core), w_lanes], wy_s.at[k], wy_r.at[ylo], device(yhi, x, k, z, core)
        )

    def w_self_copy():
        return pltpu.make_async_copy(w_ref, wt.at[slot(z, core), w_lanes], local_sem.at[0])

    same = ylo == yhi
    for k in range(2):
        to_self = jnp.logical_and(same, yhi == k)

        @pl.when(jnp.logical_not(to_self))
        def _():
            w_out_copy(k).start()

    @pl.when(same)
    def _():
        w_self_copy().start()

    def lanes(h):
        return aligned(h * HD, HD)

    def kv_copies(h):
        made = []
        for i, (src, dst) in enumerate(((k_ref, kw), (v_ref, vw))):
            made.append(remote(
                src.at[:, lanes(h)], dst.at[pl.ds(0, TOK), lanes(h)],
                kv_s.at[h, 2 * i], kv_r.at[h, 2 * i], sp_next))
            made.append(remote(
                src.at[:, lanes(h)], dst.at[pl.ds(2 * TOK, TOK), lanes(h)],
                kv_s.at[h, 2 * i + 1], kv_r.at[h, 2 * i + 1], sp_prev))
        return made

    has_prev, has_next = s > 0, s < 31

    def kv_start(h):
        copies = kv_copies(h)

        @pl.when(has_next)
        def _():
            copies[0].start()
            copies[2].start()

        @pl.when(has_prev)
        def _():
            copies[1].start()
            copies[3].start()

    def kv_wait(h):
        copies = kv_copies(h)

        @pl.when(has_prev)
        def _():
            copies[0].wait_recv()
            copies[2].wait_recv()

        @pl.when(has_next)
        def _():
            copies[1].wait_recv()
            copies[3].wait_recv()

    kv_start(0)

    def go_copy(t, left):
        rows = pl.ds(t * TILE, TILE)
        return remote(
            go_ref.at[rows, :], gall.at[rows, aligned(x * COLS, COLS)],
            ga_s.at[left, t], ga_r.at[left, t], x_at(3 if left else 1))

    def go_relay(left):
        at = gall.at[pl.ds(left * TILE, TILE), aligned((x + (1 if left else 3)) % 4 * COLS, COLS)]
        return remote(at, at, gf_s.at[left], gf_r.at[left], x_at(3 if left else 1))

    go_copy(0, 0).start()
    go_copy(1, 1).start()
    go_copy(1, 0).start()
    go_copy(0, 1).start()

    own = pl.ds(TOK, TOK)
    for side, missing in ((0, s == 0), (1, s == 31)):
        @pl.when(missing)
        def _():
            outside = pl.ds(side * 2 * TOK, TOK)
            kw[outside, :] = jnp.zeros((TOK, COLS), BF)
            vw[outside, :] = jnp.zeros((TOK, COLS), BF)
            hr[1 - side] = jnp.zeros((2, TOK, COLS), BF)

    locals_in = [
        pltpu.make_async_copy(k_ref, kw.at[own, :], local_sem.at[1]),
        pltpu.make_async_copy(v_ref, vw.at[own, :], local_sem.at[2]),
        pltpu.make_async_copy(go_ref, gall.at[:, aligned(x * COLS, COLS)], local_sem.at[3]),
    ]
    for copy in locals_in:
        copy.start()
    for copy in locals_in:
        copy.wait()

    def w_right(i):
        at = wt.at[slot((z + 8 - i) % 8, core), :]
        return remote(at, at, wr_s.at[i], wr_r.at[i], z_next)

    def w_left(i):
        at = wt.at[slot((z + i) % 8, core), :]
        return remote(at, at, wl_s.at[i], wl_r.at[i], z_prev)

    def w_core(i, z_at):
        at = wt.at[slot(z_at, core), :]
        return remote(at, at, wc_s.at[i], wc_r.at[i], partner)

    def w_ring_start():
        @pl.when(same)
        def _():
            w_self_copy().wait()

        for i in range(2):
            from_self = jnp.logical_and(same, ylo == i)

            @pl.when(jnp.logical_not(from_self))
            def _():
                remote(
                    w_ref, wt.at[slot(z, core), pl.ds(i * COLS, COLS)], wy_s.at[0], wy_r.at[i], partner
                ).wait_recv()

        w_right(0).start()
        w_left(0).start()
        w_core(0, z).start()

    def w_ring_step(i):
        w_right(i - 1).wait_recv()
        if i < 4:
            w_right(i).start()
        w_core(i, (z + 8 - i) % 8).start()
        if i < 4:
            w_left(i - 1).wait_recv()
            if i < 3:
                w_left(i).start()
            w_core(4 + i, (z + i) % 8).start()

    w_ring_start()
    kv_start(1)

    first = s * 2 - 2

    def forward(h, t):
        rows = aligned(t * TILE, TILE)
        query = q_ref[rows, lanes(h)]
        top = jnp.full((1, TILE), -3e38, F32)
        for j in range(5):
            tile_id = first + t + j
            hit = nb_ref[t, 0] == tile_id
            for i in range(1, 5):
                hit = jnp.logical_or(hit, nb_ref[t, i] == tile_id)
            hit = jnp.logical_and(hit, tile_id >= 0)
            bias = jnp.where(hit, 0.0, NEG_FILL)
            key = kw[aligned((t + j) * TILE, TILE), lanes(h)]
            block = dot_nt(key, query) * (SCALE * LOG2E) + bias
            scores[pl.ds(j * TILE, TILE), :] = block
            top = jnp.maximum(top, jnp.max(block, axis=0, keepdims=True))
        total = jnp.zeros((1, TILE), F32)
        u = h * 2 + t
        for j in range(5):
            e = jnp.exp2(scores[pl.ds(j * TILE, TILE), :] - top)
            total = total + jnp.sum(e, axis=0, keepdims=True)
            probs[u, pl.ds(j * TILE, TILE), :] = e.astype(BF)
        turned = dot_tn(
            vw[pl.ds(pl.multiple_of(t * TILE, TILE), WIN), lanes(h)], probs[u]
        )
        inv = 1.0 / total
        inv_total[u] = inv
        att[rows, pl.ds(pl.multiple_of(ylo * COLS + h * HD, HD), HD)] = (turned * inv).T.astype(BF)

    def att_copy(h):
        at = att.at[:, pl.ds(pl.multiple_of(ylo * COLS + h * HD, HD), HD)]
        return remote(at, at, at_s.at[h], at_r.at[h], y_partner)

    def fwd_step(u, carry):
        h, t = u // 2, u % 2

        @pl.when(t == 0)
        def _():
            kv_wait(h)

        @pl.when(u == 1)
        def _():
            w_ring_step(1)
            kv_start(2)

        @pl.when(u == 2)
        def _():
            go_copy(0, 0).wait_recv()
            go_relay(0).start()
            go_copy(1, 1).wait_recv()
            go_relay(1).start()

        for i in range(2, 4):
            @pl.when(u == 2 * i - 1)
            def _():
                w_ring_step(i)

        forward(h, t)

        @pl.when(t == 1)
        def _():
            att_copy(h).start()

        return carry

    lax.fori_loop(0, 2 * HEADS, fwd_step, 0)
    go_copy(1, 0).wait_recv()
    go_copy(0, 1).wait_recv()
    go_relay(0).wait_recv()
    go_relay(1).wait_recv()

    def gw_half(half):
        at = aligned(half * COLS, COLS)

        def gw_step(i, carry):
            part = dot_tn(gall[:, aligned(i * COLS, COLS)], att[:, at])
            gw[pl.ds(i * 4, 4), :, at] = part.reshape(4, PIECE, COLS)
            return carry

        lax.fori_loop(0, 4, gw_step, 0)

    gw_half(ylo)
    w_ring_step(4)
    for i in range(8):
        w_core(i, z).wait_recv()

    def gr_copy(t):
        rows = aligned(t * TILE, TILE)
        return remote(gsend.at[rows, :], grecv.at[rows, :], gr_s.at[t], gr_r.at[t], y_partner)

    def grad_step(t, carry):
        rows = aligned(t * TILE, TILE)
        block = gall[rows, :]
        gsend[rows, :] = dot_nn(block, wt[:, aligned((1 - ylo) * COLS, COLS)]).astype(BF)
        gr_copy(t).start()
        gown[rows, :] = dot_nn(block, wt[:, aligned(ylo * COLS, COLS)])
        return carry

    lax.fori_loop(0, 2, grad_step, 0)
    for h in range(HEADS):
        att_copy(h).wait_recv()
    gw_half(1 - ylo)

    def gw_cast(i, carry):
        cs[i] = gw[i * 2 + 1 - core].astype(BF)
        return carry

    lax.fori_loop(0, 8, gw_cast, 0)
    core_copy = remote(cs, cr, gc_s, gc_r, partner)
    core_copy.start()
    def g_right(i):
        return remote(rs_s.at[i], rs_r.at[i], gright_s.at[i], gright_r.at[i], z_next)

    def g_left(i):
        return remote(ls_s.at[i], ls_r.at[i], gleft_s.at[i], gleft_r.at[i], z_prev)

    def chip_sum(z_at):
        return gw[z_at * 2 + core] + cr[z_at].astype(F32)

    def g_ring_step(i):
        if i == 0:
            core_copy.wait_recv()
        if i > 0:
            g_right(i - 1).wait_recv()
        if i < 4:
            mine = chip_sum((z + 4 - i) % 8)
            if i > 0:
                mine = mine + rs_r[i - 1].astype(F32)
            rs_s[i] = mine.astype(BF)
            g_right(i).start()
        if 0 < i < 4:
            g_left(i - 1).wait_recv()
        if i < 3:
            mine = chip_sum((z + 5 + i) % 8)
            if i > 0:
                mine = mine + ls_r[i - 1].astype(F32)
            ls_s[i] = mine.astype(BF)
            g_left(i).start()


    def out_copy(i):
        return remote(osend.at[i], orecv.at[i], or_s.at[i], or_r.at[i], x_at(1 if i < 3 else 3))

    def out_part(k):
        return dot_nt(att[...], wt[aligned((x + k) % 4 * COLS, COLS), :])

    def out_send(i, part):
        osend[i] = part.astype(BF)
        out_copy(i).start()

    part = out_part(2)
    out_send(0, part[:TILE])
    out_send(3, part[TILE:])
    part = out_part(3)
    out_send(5, part[:TILE])
    held[1] = part[TILE:]
    g_ring_step(0)
    part = out_part(1)
    out_send(2, part[TILE:])
    held[0] = part[:TILE]
    oown[...] = out_part(0)

    def out_relay():
        for i in range(2):
            out_copy(3 * i).wait_recv()
            out_send(3 * i + 1, held[i] + orecv[3 * i].astype(F32))


    def halo_copy(h, i):
        side, rows = ((0, pl.ds(0, TILE)), (0, pl.ds(TILE, TILE)), (1, pl.ds(0, TOK)))[i]
        return remote(
            hs.at[side, :, rows, lanes(h)], hr.at[side, :, rows, lanes(h)], hk_s.at[h, i], hk_r.at[h, i],
            sp_next if side else sp_prev)

    def halo_send(h, i):
        side, first_row, count = ((0, 0, TILE), (0, TILE, TILE), (1, 0, TOK))[i]
        to = pl.ds(first_row, count)
        at = pl.ds(side * 2 * TOK + first_row, count)

        @pl.when(has_next if side else has_prev)
        def _():
            hs[side, 0, to, lanes(h)] = dka[at, lanes(h)].astype(BF)
            hs[side, 1, to, lanes(h)] = dva[at, lanes(h)].astype(BF)
            halo_copy(h, i).start()

    def backward(h, t):
        rows = pl.ds(t * TILE, TILE)
        u = h * 2 + t
        query = q_ref[rows, lanes(h)]
        grad = gatt[rows, lanes(h)]
        made = att[rows, pl.ds(pl.multiple_of(ylo * COLS + h * HD, HD), HD)]
        delta = jnp.sum((grad.astype(F32) * made.astype(F32)).T, axis=0, keepdims=True)
        inv = inv_total[u]
        factor = inv * SCALE
        shift = delta * factor
        inv_rows = jnp.broadcast_to(inv, (HD, TILE)).T
        grad_scaled = (grad.astype(F32) * inv_rows).astype(BF)
        turned = jnp.zeros((HD, TILE), F32)
        for j in ((0, 1, 2, 3, 4), (0, 3, 4, 1, 2))[t]:
            at = pl.ds((t + j) * TILE, TILE)
            key = kw[at, lanes(h)]
            value = vw[at, lanes(h)]
            prob = probs[u, pl.ds(j * TILE, TILE), :]
            inner = dot_nt(value, grad)
            ds = (prob.astype(F32) * (inner * factor - shift)).astype(BF)
            dk = dot_nn(ds, query)
            dv = dot_nn(prob, grad_scaled)
            if t == 0 or j == 4:
                dka[at, lanes(h)] = dk
                dva[at, lanes(h)] = dv
            else:
                dka[at, lanes(h)] += dk
                dva[at, lanes(h)] += dv
            turned = turned + dot_tn(key, ds)
            if t == 0 and j == 0:
                halo_send(h, 0)
            if t == 1 and j == 4:
                halo_send(h, 1)
                halo_send(h, 2)
        gq_ref[rows, lanes(h)] = turned.T.astype(BF)

    def gy_copy(i):
        return remote(ys.at[i], yr.at[yhi], gy_s.at[i], gy_r.at[yhi], device(i, x, ylo, z, core))

    def gy_self():
        return pltpu.make_async_copy(ys.at[ylo], yr.at[yhi], local_sem.at[4])

    def gy_start():
        z_sum = chip_sum(z) + rs_r[3].astype(F32) + ls_r[2].astype(F32)
        ys[0] = z_sum[:, :COLS]
        ys[1] = z_sum[:, COLS:]
        for i in range(2):
            to_self = jnp.logical_and(same, ylo == i)

            @pl.when(jnp.logical_not(to_self))
            def _():
                gy_copy(i).start()

        @pl.when(same)
        def _():
            gy_self().start()

    for t in range(2):
        gr_copy(t).wait_recv()
        rows = pl.ds(t * TILE, TILE)
        gatt[rows, :] = (gown[rows, :] + grecv[rows, :].astype(F32)).astype(BF)

        def bwd_step(h, carry):
            if t == 0:
                @pl.when(h == 1)
                def _():
                    g_ring_step(1)

                @pl.when(h == 2)
                def _():
                    out_relay()
            else:
                @pl.when(h == 0)
                def _():
                    g_ring_step(2)

                @pl.when(h == 2)
                def _():
                    g_ring_step(3)

            backward(h, t)
            return carry

        lax.fori_loop(0, HEADS, bwd_step, 0)

    g_ring_step(4)
    gy_start()

    for i in (1, 2, 4, 5):
        out_copy(i).wait_recv()
    for t, i, j in ((0, 1, 5), (1, 4, 2)):
        rows = pl.ds(t * TILE, TILE)
        out_ref[rows, :] = (oown[rows, :] + orecv[i].astype(F32) + orecv[j].astype(F32)).astype(BF)

    for h in range(HEADS):
        @pl.when(has_next)
        def _():
            halo_copy(h, 0).wait_recv()
            halo_copy(h, 1).wait_recv()

        @pl.when(has_prev)
        def _():
            halo_copy(h, 2).wait_recv()

        at = pl.ds(h * HD, HD)
        gk_ref[:, at] = (
            dka[own, at] + hr[0, 0, :, at].astype(F32) + hr[1, 0, :, at].astype(F32)
        ).astype(BF)
        gv_ref[:, at] = (
            dva[own, at] + hr[0, 1, :, at].astype(F32) + hr[1, 1, :, at].astype(F32)
        ).astype(BF)

    @pl.when(same)
    def _():
        gy_self().wait()

    for i in range(2):
        from_self = jnp.logical_and(same, yhi == i)

        @pl.when(jnp.logical_not(from_self))
        def _():
            remote(ys.at[i], yr.at[i], gy_s.at[i], gy_r.at[i], partner).wait_recv()

    gw_ref[...] = yr[0] + yr[1]

    for k in range(2):
        to_self = jnp.logical_and(same, yhi == k)

        @pl.when(jnp.logical_not(to_self))
        def _():
            w_out_copy(k).wait_send()

    for i in range(2):
        to_self = jnp.logical_and(same, ylo == i)

        @pl.when(jnp.logical_not(to_self))
        def _():
            gy_copy(i).wait_send()

    for h in range(HEADS):
        copies = kv_copies(h)

        @pl.when(has_next)
        def _():
            for copy in (copies[0], copies[2], halo_copy(h, 2)):
                copy.wait_send()

        @pl.when(has_prev)
        def _():
            for copy in (copies[1], copies[3], halo_copy(h, 0), halo_copy(h, 1)):
                copy.wait_send()

        att_copy(h).wait_send()
    for t in range(2):
        gr_copy(t).wait_send()
        go_copy(t, 0).wait_send()
        go_copy(t, 1).wait_send()
        go_relay(t).wait_send()
    for i in range(6):
        out_copy(i).wait_send()
    for i in range(4):
        w_right(i).wait_send()
        g_right(i).wait_send()
    for i in range(3):
        w_left(i).wait_send()
        g_left(i).wait_send()
    for i in range(8):
        w_core(i, z).wait_send()
    core_copy.wait_send()


def deliver(*refs):
    for source, target in zip(refs[:5], refs[5:]):
        target[...] = source[...]


def local(queries, keys, values, w_out, grad_out, neighbors):
    vmem = lambda shape, dtype: pltpu.VMEM(shape, dtype)
    dma = lambda *shape: pltpu.SemaphoreType.DMA(shape)
    big = jax.ShapeDtypeStruct((TOK, COLS), BF)
    anywhere = pl.BlockSpec(memory_space=pl.ANY)
    whole = pl.BlockSpec(memory_space=pltpu.VMEM)
    out, gq, gk, gv, gwt = pl.pallas_call(
        kernel,
        out_shape=(big, big, big, big, jax.ShapeDtypeStruct((PIECE, COLS), F32)),
        in_specs=[pl.BlockSpec(memory_space=pltpu.SMEM), whole, anywhere, anywhere, anywhere, anywhere],
        out_specs=[whole] * 5,
        scratch_shapes=[
            vmem((WIDE, COLS), BF), vmem((WIDE, COLS), BF),
            vmem((TOK, 4 * COLS), BF), vmem((4 * COLS, 2 * COLS), BF), vmem((TOK, 2 * COLS), BF),
            vmem((WIN, TILE), F32), vmem((2 * HEADS, WIN, TILE), BF), vmem((2 * HEADS, 1, TILE), F32),
            vmem((TOK, COLS), BF), vmem((TOK, COLS), BF), vmem((TOK, COLS), F32), vmem((TOK, COLS), BF),
            vmem((6, TILE, COLS), BF), vmem((6, TILE, COLS), BF), vmem((TOK, COLS), F32), vmem((2, TILE, COLS), F32),
            vmem((16, PIECE, 2 * COLS), F32),
            vmem((8, PIECE, 2 * COLS), BF), vmem((8, PIECE, 2 * COLS), BF),
            vmem((4, PIECE, 2 * COLS), BF), vmem((4, PIECE, 2 * COLS), BF),
            vmem((3, PIECE, 2 * COLS), BF), vmem((3, PIECE, 2 * COLS), BF),
            vmem((2, PIECE, COLS), F32), vmem((2, PIECE, COLS), F32),
            vmem((WIDE, COLS), F32), vmem((WIDE, COLS), F32),
            vmem((2, 2, TOK, COLS), BF), vmem((2, 2, TOK, COLS), BF),
            dma(5), dma(2), dma(2), dma(4), dma(4), dma(3), dma(3), dma(8), dma(8),
            dma(3, 4), dma(3, 4), dma(2, 2), dma(2, 2), dma(2), dma(2), dma(3), dma(3), dma(2), dma(2), dma(6), dma(6),
            pltpu.SemaphoreType.DMA, pltpu.SemaphoreType.DMA, dma(4), dma(4), dma(3), dma(3), dma(2), dma(2),
            dma(3, 3), dma(3, 3),
        ],
        compiler_params=pltpu.CompilerParams(
            collective_id=0, has_side_effects=True, vmem_limit_bytes=62 * 2**20
        ),
        name="block",
    )(neighbors, queries, keys, values, w_out.T, grad_out)
    out, gq, gk, gv, gwt = pl.pallas_call(
        deliver,
        out_shape=(big, big, big, big, jax.ShapeDtypeStruct((PIECE, COLS), F32)),
        in_specs=[whole] * 5,
        out_specs=[whole] * 5,
        name="deliver",
    )(out, gq, gk, gv, gwt)
    return (out, gq, gk, gv, gwt.T)


def solution(mesh):
    placed = (
        P("sp", "fsdp"),
        P("sp", "fsdp"),
        P("sp", "fsdp"),
        P("fsdp", "sp"),
        P("sp", "fsdp"),
        P("sp", None),
    )
    return jax.shard_map(
        local,
        mesh=mesh,
        in_specs=placed,
        out_specs=(
            P("sp", "fsdp"),
            P("sp", "fsdp"),
            P("sp", "fsdp"),
            P("sp", "fsdp"),
            P("fsdp", "sp"),
        ),
        check_vma=False,
    )
```

profile of v0, /device:TPU:1, one launch (start us, length us, event | category | flops | bytes accessed | tf_op | source)
XLA Modules:
  0.0 91.2 jit_solution(2347143609454674171)
XLA Ops:
  0.6 87.4 %block.1 = (bf16[768,384]{1,0:T(8,128)(2,1)}, bf16[768,384]{1,0:T(8,128)(2,1)}, bf16[768,384]{1,0:T(8,128)(2,1)}, bf16[768,384]{1,0:T(8,128)(2,1)}, f32[96,384]{1,0:T(8,128)}) custom-call(s32[2,5]{1,0:T(2,128)} %nb_ref.1, bf16[768,384]{1,0:T(8,128)(2,1)} %q_ref.1, bf16[768,384]{1,0:T(8,128)(2,1)} %k_ref.1, bf16[768,384]{1,0:T(8,128)(2,1)} %v_ref.1, ...), custom_call_target="tpu_custom_call" | custom-call | tf_op jit(solution)/shard_map/block/pallas_call | solution.py:602
  88.0 3.2 %deliver.1 = (bf16[768,384]{1,0:T(8,128)(2,1)}, bf16[768,384]{1,0:T(8,128)(2,1)}, bf16[768,384]{1,0:T(8,128)(2,1)}, bf16[768,384]{1,0:T(8,128)(2,1)}, f32[96,384]{1,0:T(8,128)}) custom-call(bf16[768,384]{1,0:T(8,128)(2,1)} %get-tuple-element.15.refs_0_, bf16[768,384]{1,0:T(8,128)(2,1)} %get-tuple-element.16.refs_1_, ...), custom_call_target="tpu_custom_call" | custom-call | tf_op jit(solution)/shard_map/deliver/pallas_call | solution.py:630
where the time goes:
time: 91.3 us; the launch traced here: 91.2 us
  Pallas kernels  90.5 us (99%)
    pallas_call x1, Pallas kernels, local(): pl.pallas_call(kernel, out_shape=(big, big, big, big, jax.ShapeDtypeStruc...  87.4 us
    pallas_call x1, Pallas kernels, local(): pl.pallas_call(deliver, out_shape=(big, big, big, big, jax.ShapeDtypeStru...  3.17 us

commit v1 on v0

--- a/solution.py
+++ b/solution.py
@@ -15,6 +15,7 @@
 WIN = 5 * TILE
 WIDE = 6 * TILE
 PIECE = 96
+HALF = 48
 MESH = pl.DeviceIdType.MESH
 SCALE = 1.0 / math.sqrt(HD)
 LOG2E = 1.4426950408889634
@@ -187,12 +188,18 @@
     for copy in locals_in:
         copy.wait()
 
+    def w_rows(z_at, i, half):
+        start = (z_at * 2 + core) * PIECE
+        if i < 3:
+            return pl.ds(pl.multiple_of(start, 32), PIECE)
+        return pl.ds(pl.multiple_of(start + half * HALF, 16), HALF)
+
     def w_right(i):
-        at = wt.at[slot((z + 8 - i) % 8, core), :]
+        at = wt.at[w_rows((z + 8 - i) % 8, i, 0), :]
         return remote(at, at, wr_s.at[i], wr_r.at[i], z_next)
 
     def w_left(i):
-        at = wt.at[slot((z + i) % 8, core), :]
+        at = wt.at[w_rows((z + i) % 8, i, 1), :]
         return remote(at, at, wl_s.at[i], wl_r.at[i], z_prev)
 
     def w_core(i, z_at):
@@ -221,12 +228,11 @@
         w_right(i - 1).wait_recv()
         if i < 4:
             w_right(i).start()
-        w_core(i, (z + 8 - i) % 8).start()
+            w_core(i, (z + 8 - i) % 8).start()
+        w_left(i - 1).wait_recv()
         if i < 4:
-            w_left(i - 1).wait_recv()
-            if i < 3:
-                w_left(i).start()
-            w_core(4 + i, (z + i) % 8).start()
+            w_left(i).start()
+        w_core(4 + i if i < 4 else 4, (z + i) % 8).start()
 
     w_ring_start()
     kv_start(1)
@@ -342,11 +348,11 @@
     lax.fori_loop(0, 8, gw_cast, 0)
     core_copy = remote(cs, cr, gc_s, gc_r, partner)
     core_copy.start()
-    def g_right(i):
-        return remote(rs_s.at[i], rs_r.at[i], gright_s.at[i], gright_r.at[i], z_next)
-
-    def g_left(i):
-        return remote(ls_s.at[i], ls_r.at[i], gleft_s.at[i], gleft_r.at[i], z_prev)
+    def g_copy(i, left):
+        sent, landed = (ls_s, ls_r) if left else (rs_s, rs_r)
+        send, recv = (gleft_s, gleft_r) if left else (gright_s, gright_r)
+        at = (i, pl.ds(left * HALF, HALF)) if i == 0 else (i,)
+        return remote(sent.at[at], landed.at[at], send.at[i], recv.at[i], z_prev if left else z_next)
 
     def chip_sum(z_at):
         return gw[z_at * 2 + core] + cr[z_at].astype(F32)
@@ -354,23 +360,19 @@
     def g_ring_step(i):
         if i == 0:
             core_copy.wait_recv()
-        if i > 0:
-            g_right(i - 1).wait_recv()
-        if i < 4:
-            mine = chip_sum((z + 4 - i) % 8)
+        for left in range(2):
+            sent, landed = (ls_s, ls_r) if left else (rs_s, rs_r)
+            half = pl.ds(left * HALF, HALF)
             if i > 0:
-                mine = mine + rs_r[i - 1].astype(F32)
-            rs_s[i] = mine.astype(BF)
-            g_right(i).start()
-        if 0 < i < 4:
-            g_left(i - 1).wait_recv()
-        if i < 3:
-            mine = chip_sum((z + 5 + i) % 8)
-            if i > 0:
-                mine = mine + ls_r[i - 1].astype(F32)
-            ls_s[i] = mine.astype(BF)
-            g_left(i).start()
-
+                g_copy(i - 1, left).wait_recv()
+            if i < 4:
+                mine = chip_sum((z + 4 + i if left else z + 4 - i) % 8)
+                if i > 1:
+                    mine = mine + landed[i - 1].astype(F32)
+                sent[i] = mine.astype(BF)
+                if i == 1:
+                    sent[1, half] = (mine[left * HALF:(left + 1) * HALF] + landed[0, half].astype(F32)).astype(BF)
+                g_copy(i, left).start()
 
     def out_copy(i):
         return remote(osend.at[i], orecv.at[i], or_s.at[i], or_r.at[i], x_at(1 if i < 3 else 3))
@@ -460,7 +462,7 @@
         return pltpu.make_async_copy(ys.at[ylo], yr.at[yhi], local_sem.at[4])
 
     def gy_start():
-        z_sum = chip_sum(z) + rs_r[3].astype(F32) + ls_r[2].astype(F32)
+        z_sum = chip_sum(z) + rs_r[3].astype(F32) + ls_r[3].astype(F32)
         ys[0] = z_sum[:, :COLS]
         ys[1] = z_sum[:, COLS:]
         for i in range(2):
@@ -474,33 +476,44 @@
         def _():
             gy_self().start()
 
-    for t in range(2):
+    def grad_ready(t):
         gr_copy(t).wait_recv()
         rows = pl.ds(t * TILE, TILE)
         gatt[rows, :] = (gown[rows, :] + grecv[rows, :].astype(F32)).astype(BF)
 
-        def bwd_step(h, carry):
-            if t == 0:
-                @pl.when(h == 1)
-                def _():
-                    g_ring_step(1)
-
-                @pl.when(h == 2)
-                def _():
-                    out_relay()
-            else:
-                @pl.when(h == 0)
-                def _():
-                    g_ring_step(2)
-
-                @pl.when(h == 2)
-                def _():
-                    g_ring_step(3)
-
-            backward(h, t)
-            return carry
-
-        lax.fori_loop(0, HEADS, bwd_step, 0)
+    def bwd_step(i, carry):
+        h = jnp.where(i < 4, i % 2, 2)
+        t = jnp.where(i < 4, i // 2, i - 4)
+
+        @pl.when(i == 0)
+        def _():
+            grad_ready(0)
+
+        @pl.when(i == 1)
+        def _():
+            g_ring_step(1)
+
+        @pl.when(i == 2)
+        def _():
+            grad_ready(1)
+            out_relay()
+            g_ring_step(2)
+
+        @pl.when(i == 3)
+        def _():
+            g_ring_step(3)
+
+        @pl.when(t == 0)
+        def _():
+            backward(h, 0)
+
+        @pl.when(t == 1)
+        def _():
+            backward(h, 1)
+
+        return carry
+
+    lax.fori_loop(0, 2 * HEADS, bwd_step, 0)
 
     g_ring_step(4)
     gy_start()
@@ -579,10 +592,9 @@
         out_copy(i).wait_send()
     for i in range(4):
         w_right(i).wait_send()
-        g_right(i).wait_send()
-    for i in range(3):
         w_left(i).wait_send()
-        g_left(i).wait_send()
+        g_copy(i, 0).wait_send()
+        g_copy(i, 1).wait_send()
     for i in range(8):
         w_core(i, z).wait_send()
     core_copy.wait_send()
@@ -613,13 +625,13 @@
             vmem((16, PIECE, 2 * COLS), F32),
             vmem((8, PIECE, 2 * COLS), BF), vmem((8, PIECE, 2 * COLS), BF),
             vmem((4, PIECE, 2 * COLS), BF), vmem((4, PIECE, 2 * COLS), BF),
-            vmem((3, PIECE, 2 * COLS), BF), vmem((3, PIECE, 2 * COLS), BF),
+            vmem((4, PIECE, 2 * COLS), BF), vmem((4, PIECE, 2 * COLS), BF),
             vmem((2, PIECE, COLS), F32), vmem((2, PIECE, COLS), F32),
             vmem((WIDE, COLS), F32), vmem((WIDE, COLS), F32),
             vmem((2, 2, TOK, COLS), BF), vmem((2, 2, TOK, COLS), BF),
-            dma(5), dma(2), dma(2), dma(4), dma(4), dma(3), dma(3), dma(8), dma(8),
+            dma(5), dma(2), dma(2), dma(4), dma(4), dma(4), dma(4), dma(8), dma(8),
             dma(3, 4), dma(3, 4), dma(2, 2), dma(2, 2), dma(2), dma(2), dma(3), dma(3), dma(2), dma(2), dma(6), dma(6),
-            pltpu.SemaphoreType.DMA, pltpu.SemaphoreType.DMA, dma(4), dma(4), dma(3), dma(3), dma(2), dma(2),
+            pltpu.SemaphoreType.DMA, pltpu.SemaphoreType.DMA, dma(4), dma(4), dma(4), dma(4), dma(2), dma(2),
             dma(3, 3), dma(3, 3),
         ],
         compiler_params=pltpu.CompilerParams(

time: 91.3 us -> 90.6 us (level)
  no operation moved by 1% of the time
where the time goes in v1:
time: 90.6 us; the launch traced here: 90.3 us
  Pallas kernels  89.7 us (99%)
    pallas_call x1, Pallas kernels, local(): pl.pallas_call(kernel, out_shape=(big, big, big, big, jax.ShapeDtypeStruc...  86.5 us
    pallas_call x1, Pallas kernels, local(): pl.pallas_call(deliver, out_shape=(big, big, big, big, jax.ShapeDtypeStru...  3.17 us

profile of v1, /device:TPU:1, one launch (start us, length us, event | category | flops | bytes accessed | tf_op | source)
XLA Modules:
  0.0 90.3 jit_solution(11221992645267227183)
XLA Ops:
  0.6 86.5 %block.1 = (bf16[768,384]{1,0:T(8,128)(2,1)}, bf16[768,384]{1,0:T(8,128)(2,1)}, bf16[768,384]{1,0:T(8,128)(2,1)}, bf16[768,384]{1,0:T(8,128)(2,1)}, f32[96,384]{1,0:T(8,128)}) custom-call(s32[2,5]{1,0:T(2,128)} %nb_ref.1, bf16[768,384]{1,0:T(8,128)(2,1)} %q_ref.1, bf16[768,384]{1,0:T(8,128)(2,1)} %k_ref.1, bf16[768,384]{1,0:T(8,128)(2,1)} %v_ref.1, ...), custom_call_target="tpu_custom_call" | custom-call | tf_op jit(solution)/shard_map/block/pallas_call | solution.py:614
  87.1 3.2 %deliver.1 = (bf16[768,384]{1,0:T(8,128)(2,1)}, bf16[768,384]{1,0:T(8,128)(2,1)}, bf16[768,384]{1,0:T(8,128)(2,1)}, bf16[768,384]{1,0:T(8,128)(2,1)}, f32[96,384]{1,0:T(8,128)}) custom-call(bf16[768,384]{1,0:T(8,128)(2,1)} %get-tuple-element.15.refs_0_, bf16[768,384]{1,0:T(8,128)(2,1)} %get-tuple-element.16.refs_1_, ...), custom_call_target="tpu_custom_call" | custom-call | tf_op jit(solution)/shard_map/deliver/pallas_call | solution.py:642

commit v2 on v1

--- a/solution.py
+++ b/solution.py
@@ -280,8 +280,8 @@
 
         @pl.when(u == 1)
         def _():
+            kv_start(2)
             w_ring_step(1)
-            kv_start(2)
 
         @pl.when(u == 2)
         def _():

time: 90.6 us -> 90 us (level)
  no operation moved by 1% of the time
where the time goes in v2:
time: 90 us; the launch traced here: 89.8 us
  Pallas kernels  89.1 us (99%)
    pallas_call x1, Pallas kernels, local(): pl.pallas_call(kernel, out_shape=(big, big, big, big, jax.ShapeDtypeStruc...  86 us
    pallas_call x1, Pallas kernels, local(): pl.pallas_call(deliver, out_shape=(big, big, big, big, jax.ShapeDtypeStru...  3.17 us

profile of v2, /device:TPU:1, one launch (start us, length us, event | category | flops | bytes accessed | tf_op | source)
XLA Modules:
  0.0 89.8 jit_solution(10377395642064898805)
XLA Ops:
  0.6 86.0 %block.1 = (bf16[768,384]{1,0:T(8,128)(2,1)}, bf16[768,384]{1,0:T(8,128)(2,1)}, bf16[768,384]{1,0:T(8,128)(2,1)}, bf16[768,384]{1,0:T(8,128)(2,1)}, f32[96,384]{1,0:T(8,128)}) custom-call(s32[2,5]{1,0:T(2,128)} %nb_ref.1, bf16[768,384]{1,0:T(8,128)(2,1)} %q_ref.1, bf16[768,384]{1,0:T(8,128)(2,1)} %k_ref.1, bf16[768,384]{1,0:T(8,128)(2,1)} %v_ref.1, ...), custom_call_target="tpu_custom_call" | custom-call | tf_op jit(solution)/shard_map/block/pallas_call | solution.py:614
  86.6 3.2 %deliver.1 = (bf16[768,384]{1,0:T(8,128)(2,1)}, bf16[768,384]{1,0:T(8,128)(2,1)}, bf16[768,384]{1,0:T(8,128)(2,1)}, bf16[768,384]{1,0:T(8,128)(2,1)}, f32[96,384]{1,0:T(8,128)}) custom-call(bf16[768,384]{1,0:T(8,128)(2,1)} %get-tuple-element.15.refs_0_, bf16[768,384]{1,0:T(8,128)(2,1)} %get-tuple-element.16.refs_1_, ...), custom_call_target="tpu_custom_call" | custom-call | tf_op jit(solution)/shard_map/deliver/pallas_call | solution.py:642
